TPU v7x, 256 devices: a whole 4x4x8 slice. The times are simulated.
256 devices in a mesh: chan: 64 (over y, x, z_lo, core), feed: 4 (over z_hi).
Axes of the slice: x: 4, y: 4, z: 8 (z_hi: 4, z_lo: 2; z = z_hi * 2 + z_lo), core: 2. Of those that a mesh axis runs over, the one named last changes fastest.
Arguments:
- voltages: int32 [2048, 64, 2048], P('chan', 'feed'), may hold values from -128 to 127
- taper: float32 [4, 2048], replicated, may hold values from -3 to 3
- gains: int32 [2048, 128], P('chan'), may hold values from 16 to 79
Outputs:
- visibility: bfloat16 [128, 2, 2048, 2048], P('chan', None, 'feed')
All inputs are finite; a program needn't handle non-finite values.
Results may differ from a plain program's by a relative error of at most 0.0057.
Values may be sent and summed in bfloat16 or wider, within the bound.
A program may use at most 64 MiB of HBM per device.

v0:
```python
import math

import jax
import jax.numpy as jnp
from jax import lax
from jax.sharding import PartitionSpec as P


def shifted(value, axis, steps):
    count = lax.axis_size(axis)
    leading, last = (max(0, -steps), min(count, count - steps))
    return lax.ppermute(value, axis, [(source, source + steps) for source in range(leading, last)])


def dft_table(points, count):
    positions = jnp.arange(points, dtype=jnp.int32)
    orders = jnp.arange(count, dtype=jnp.int32) + 1
    phase = positions[:, None] * orders[None, :] % points
    angle = phase.astype(jnp.float32) * (2.0 * math.pi / points)
    norm = 1.0 / math.sqrt(points)
    pair = jnp.stack([jnp.cos(angle) * norm, -jnp.sin(angle) * norm], axis=-1)
    return pair.reshape(points, 2 * count)


def transform(filtered, table):
    return jnp.einsum(
        "isn,nk->ksi",
        filtered,
        table,
        preferred_element_type=jnp.float32,
        precision=lax.Precision.HIGHEST,
    )


def correlate(piece, first_row, row_count):
    own_rows = lax.dynamic_slice_in_dim(piece, first_row, row_count, 3)
    real_part = own_rows[:, 0]
    imag_part = own_rows[:, 1]
    left = jnp.stack(
        [jnp.stack([real_part, imag_part], 1), jnp.stack([imag_part, -real_part], 1)], 1
    )
    return jnp.einsum("cotsr,ctsq->corq", left, piece, preferred_element_type=jnp.float32)


def arrange(moved, sources, chan_local, spec_count, in_dev):
    laid = moved.reshape(sources, chan_local, 2, spec_count, in_dev)
    return laid.transpose(1, 2, 3, 0, 4).reshape(chan_local, 2, spec_count, sources * in_dev)


def on_device(voltages, taper, gains):
    in_dev, spec_dev, points = voltages.shape
    taps = taper.shape[0]
    channels = gains.shape[1]
    table = dft_table(points, channels)
    samples = voltages.astype(jnp.float32)
    narrow = samples.astype(jnp.bfloat16)
    earlier = shifted(narrow[:, spec_dev - (taps - 1) :, :], "feed", 1)
    extended = jnp.concatenate([earlier.astype(jnp.float32), samples], axis=1)
    total = jnp.zeros((in_dev, spec_dev, points), jnp.float32)
    for tap in range(taps):
        total = total + taper[tap][None, None, :] * extended[:, tap : tap + spec_dev, :]
    spec = transform(total * (1.0 / 64.0), table)
    spec = spec.reshape(channels, 2, spec_dev, in_dev)
    factor = (gains.astype(jnp.float32) / 64.0).T
    signals = (spec * factor[:, None, None, :]).astype(jnp.bfloat16)
    feeds = lax.axis_size("feed")
    chan_count = lax.axis_size("chan")
    chan_local = channels // chan_count
    inputs_all = in_dev * chan_count
    row_count = inputs_all // feeds
    first_row = lax.axis_index("feed") * row_count
    spectra_all = spec_dev * feeds
    flat = signals.reshape(channels, 2, spec_dev * in_dev)
    assembled = lax.all_gather(flat, "feed", axis=2, tiled=True)
    outgoing = assembled.reshape(chan_count, chan_local, 2, spectra_all * in_dev)
    moved = lax.all_to_all(outgoing, "chan", split_axis=0, concat_axis=0, tiled=True)
    turned = arrange(moved, chan_count, chan_local, spectra_all, in_dev)
    summed = correlate(turned, first_row, row_count)
    return (summed * (1.0 / spectra_all)).astype(jnp.bfloat16)


def solution(mesh):
    placed = (P("chan", "feed", None), P(), P("chan", None))
    return jax.shard_map(
        on_device,
        mesh=mesh,
        in_specs=placed,
        out_specs=P("chan", None, "feed", None),
        check_vma=False,
    )
```

profile of v0, /device:TPU:1, one launch (start us, length us, event | category | flops | bytes accessed | tf_op | source)
XLA Modules:
  0.0 140.4 jit_solution(11051425188840771381)
XLA Ops:
  6.5 0.0 copy-start.2
  6.5 0.0 all-gather.2.cloned.1.call-start
  6.5 4.6 %copy_convert_fusion = f32[32,16,2048]{2,0,1:T(8,128)S(1)} fusion(s32[32,16,2048]{2,1,0:T(8,128)} %param.3), kind=kLoop, calls=%fused_computation.18 | loop fusion | flops 1048576 | bytes 8388608 | tf_op jit(solution)/shard_map/convert_element_type | solution.py:55
  11.2 0.0 copy-start
  11.2 2.0 %copy-done = f32[32,16,2048]{2,0,1:T(8,128)} copy-done((f32[32,16,2048]{2,0,1:T(8,128)}, f32[32,16,2048]{2,0,1:T(8,128)S(1)}, u32[]{:S(2)}) %copy-start) | copy-done | bytes 4194328
  13.2 5.9 %collective-permute-start = (bf16[32,3,2048]{2,0,1:T(8,128)(2,1)S(1)}, bf16[32,3,2048]{2,0,1:T(8,128)(2,1)S(1)}, u32[]{:S(2)}, u32[]{:S(2)}) collective-permute-start(bf16[32,3,2048]{2,0,1:T(8,128)(2,1)S(1)} %slice.88), channel_id=1, source_target_pairs={{0,1},{1,2},{2,3},{4,5},{5,6},{6,7},{8,9},{9,10},{10,11},{12,13},{... | collective-permute-start | bytes 1179656 | tf_op jit(solution)/shard_map/ppermute | solution.py:12
  19.2 0.0 copy-done.2
  19.2 0.1 copy.34
  19.4 4.2 %cosine_multiply_fusion = (f32[2048,128,1]{1,0,2:T(8,128)S(1)}, f32[2048,128,1]{1,0,2:T(8,128)S(1)}) fusion(s32[128]{0:T(128)S(1)} %iota_add_fusion), kind=kLoop, calls=%fused_computation.35 | loop fusion | flops 4456448 | bytes 2097664 | tf_op jit(solution)/shard_map/mul | solution.py:21
  23.5 0.1 pad_maximum_fusion.1
  23.7 0.0 copy-start.1
  23.7 2.4 %copy.30 = f32[2048,128,2]{0,2,1:T(2,128)} copy(f32[2048,128,2]{1,0,2:T(8,128)S(1)} %pad_maximum_fusion.1) | data formatting | bytes 4194304 | tf_op jit(solution)/shard_map/stack | solution.py:21
  26.1 2.7 %reshape.133 = f32[2048,256]{0,1:T(8,128)S(1)} reshape(f32[2048,128,2]{0,2,1:T(2,128)} %copy.30) | data formatting | bytes 4194304 | tf_op jit(solution)/shard_map/reshape | solution.py:22
  28.8 0.0 copy-done.1
  28.9 0.0 collective-permute-done
  28.9 0.1 convert_element_type.38
  29.0 8.6 %fusion.22 = f32[256,16,32]{0,2,1:T(8,128)S(1)} fusion(f32[32,16,2048]{2,0,1:T(8,128)} %copy-done, f32[32,3,2048]{2,0,1:T(8,128)S(1)} %convert_element_type.38, f32[2048]{0:T(1024)S(1)} %bitcast.42, f32[2048]{0:T(1024)S(1)} %bitcast.43, f32[2048]{0:T(1024)S(1)} %bitcast.41, f32[2048]{0:T(1024)S(1)} %bitcast.40, f32[2048,256]{0,1:T(8,128)S(1)} %reshape.133), kind=kOutput, calls=%fused_computation.30 | convolution fusion | flops 3232759808 | bytes 7634944 | tf_op jit(solution)/shard_map/isn,nk->ksi/dot_general | solution.py:26
  37.5 1.3 copy.33
  38.9 1.2 reshape.134
  40.0 1.0 multiply_convert_fusion
  41.0 0.0 all-gather.2.cloned.1.call-update
  41.0 50.5 %all-gather.2.cloned.1.call-done = bf16[128,2,2048]{2,1,0:T(2,128)(2,1)} async-done(((bf16[128,2,512]{2,1,0:T(2,128)(2,1)}), bf16[128,2,2048]{2,1,0:T(2,128)(2,1)}) %all-gather.2.cloned.1.call-update) | async-done | bytes 1048592 | tf_op jit(solution)/shard_map/all_gather | solution.py:74
  91.6 8.3 %all-to-all-start = ((bf16[64,2,2,2048]{3,2,1,0:T(2,128)(2,1)}), bf16[64,2,2,2048]{3,2,1,0:T(2,128)(2,1)S(1)}, u32[]{:S(2)}, u32[]{:S(2)}) async-start(bf16[64,2,2,2048]{3,2,1,0:T(2,128)(2,1)} %bitcast.38), calls=%async_computation | async-start | bytes 2097152 | tf_op jit(solution)/shard_map/all_to_all | solution.py:76
  99.9 18.3 %all-to-all-done = bf16[64,2,2,2048]{3,2,1,0:T(2,128)(2,1)S(1)} async-done(((bf16[64,2,2,2048]{3,2,1,0:T(2,128)(2,1)}), bf16[64,2,2,2048]{3,2,1,0:T(2,128)(2,1)S(1)}, u32[]{:S(2)}, u32[]{:S(2)}) %all-to-all-start) | async-done | bytes 1048608 | tf_op jit(solution)/shard_map/all_to_all | solution.py:76
  118.2 1.5 %copy.35 = bf16[64,2,2,2048]{0,3,2,1:T(8,128)(2,1)S(1)} copy(bf16[64,2,2,2048]{3,2,1,0:T(2,128)(2,1)S(1)} %all-to-all-done) | data formatting | bytes 2097152 | tf_op jit(solution)/shard_map/all_to_all | solution.py:76
  119.7 4.9 %copy.36 = bf16[2,2,64,64,32]{2,4,3,1,0:T(8,128)(2,1)} copy(bf16[2,2,64,64,32]{3,4,2,1,0:T(8,128)(2,1)S(1)} %bitcast.34) | data formatting | bytes 2097152 | tf_op jit(solution)/shard_map/transpose | solution.py:47
  124.6 1.1 constant_dynamic-slice_fusion
  125.7 0.2 copy.45
  126.0 7.6 %fusion = bf16[2,2,512,2048]{3,2,1,0:T(8,128)(2,1)} fusion(bf16[2,2,64,2048,1]{2,3,1,4,0:T(8,128)(2,1)} %bitcast.36, bf16[2,1,2,64,512]{4,3,2,1,0:T(8,128)(2,1)S(1)} %maximum_bitcast_fusion, bf16[2,1,2,64,512]{4,3,2,1,0:T(8,128)(2,1)S(1)} %bitcast.37), kind=kOutput, calls=%fused_computation.1 | convolution fusion | flops 1082392576 | bytes 9961472 | tf_op jit(solution)/shard_map/cotsr,ctsq->corq/dot_general | solution.py:42
  (7 shorter events, 0.1 us)
Async XLA Ops:
  6.5 12.7 %copy-start.2 = (s32[32,128]{1,0:T(8,128)S(1)}, s32[32,128]{1,0:T(8,128)}, u32[]{:S(2)}) copy-start(s32[32,128]{1,0:T(8,128)} %param.5) | copy-start | bytes 49156
  6.5 85.1 %all-gather.2.cloned.1.call-start = ((), (), s32[]{:S(2)}) async-start(), calls=%async_computation.1 | async-start | bytes 1310720 | tf_op jit(solution)/shard_map/all_gather | solution.py:74
  11.2 2.0 %copy-start = (f32[32,16,2048]{2,0,1:T(8,128)}, f32[32,16,2048]{2,0,1:T(8,128)S(1)}, u32[]{:S(2)}) copy-start(f32[32,16,2048]{2,0,1:T(8,128)S(1)} %copy_convert_fusion) | copy-start | bytes 12582916
  13.2 15.6 %collective-permute-start = (bf16[32,3,2048]{2,0,1:T(8,128)(2,1)S(1)}, bf16[32,3,2048]{2,0,1:T(8,128)(2,1)S(1)}, u32[]{:S(2)}, u32[]{:S(2)}) collective-permute-start(bf16[32,3,2048]{2,0,1:T(8,128)(2,1)S(1)} %slice.88), channel_id=1, source_target_pairs={{0,1},{1,2},{2,3},{4,5},{5,6},{6,7},{8,9},{9,10},{10,11},{12,13},{... | collective-permute-start | bytes 1179656 | tf_op jit(solution)/shard_map/ppermute | solution.py:12
  23.7 5.1 %copy-start.1 = (f32[4,2048]{1,0:T(4,128)S(1)}, f32[4,2048]{1,0:T(4,128)}, u32[]{:S(2)}) copy-start(f32[4,2048]{1,0:T(4,128)} %param.4) | copy-start | bytes 98308
  91.6 26.6 %all-to-all-start = ((bf16[64,2,2,2048]{3,2,1,0:T(2,128)(2,1)}), bf16[64,2,2,2048]{3,2,1,0:T(2,128)(2,1)S(1)}, u32[]{:S(2)}, u32[]{:S(2)}) async-start(bf16[64,2,2,2048]{3,2,1,0:T(2,128)(2,1)} %bitcast.38), calls=%async_computation | async-start | bytes 2097152 | tf_op jit(solution)/shard_map/all_to_all | solution.py:76
Sparse Core Ops, SparseCore 0:
  41.2 50.3 all-gather.1
where the time goes:
time: 141 us; the launch traced here: 140 us
  waiting for transfers between devices  68.9 us (49%)
  local copies, waits for them, and re-layouts  17.5 us (12%)
  matrix products  16.2 us (11%)
  starting transfers between devices  14.2 us (10%)
  between operations  13.6 us (10%)
  other arithmetic  10 us (7%)
    all_gather x1, waiting for transfers between devices, on_device(): assembled = lax.all_gather(flat, 'feed', axis=2, tiled=True)  50.5 us
    all_to_all x1, waiting for transfers between devices, on_device(): lax.all_to_all(outgoing, 'chan', split_axis=0, concat_axis=0, tiled=True)  18.3 us
    dot_general x1, matrix products, transform(): jnp.einsum('isn,nk->ksi', filtered, table, preferred_element_type=jnp.flo...  8.59 us
    all_to_all x1, starting transfers between devices, on_device(): lax.all_to_all(outgoing, 'chan', split_axis=0, concat_axis=0, tiled=True)  8.29 us
    dot_general x1, matrix products, correlate(): jnp.einsum('cotsr,ctsq->corq', left, piece, preferred_element_type=jnp.fl...  7.58 us
    ppermute x1, starting transfers between devices, shifted(): lax.ppermute(value, axis, [(source, source + steps) for source in range(l...  5.93 us
    transpose x1, local copies, waits for them, and re-layouts, arrange(): laid.transpose(1, 2, 3, 0, 4)  4.93 us
    convert_element_type x1, other arithmetic, on_device(): samples = voltages.astype(jnp.float32)  4.63 us
  transfers between devices with their start and end apart: 3, of which 2 were waited for; matrix products, arithmetic and copies ran while one was open for 7% of the time, Pallas kernels for 0%

commit v1 on v0

v1 whole, which is shorter than its diff:
```python
import functools
import math

import jax
import jax.numpy as jnp
import numpy as np
from jax import lax
from jax.experimental import pallas as pl
from jax.experimental.pallas import tpu as pltpu
from jax.sharding import PartitionSpec as P

MESH = pl.DeviceIdType.MESH
F32, BF16 = jnp.float32, jnp.bfloat16

POINTS = 2048
HALF = POINTS // 2
CHANNELS = 128
IN_DEV = 32
SPECS = 16
TAPS = 4
COLUMNS = 16
RING = 8
SOURCES = 2 * COLUMNS
TILE = 16
LANES = 128
CHUNKS = 4
PIECE = SOURCES // CHUNKS


def tile_channel():
    parity, place = np.divmod(np.arange(2 * SOURCES), SOURCES)
    column, core = np.divmod(place, 2)
    return 2 * (column * 4 + parity * 2 + core)


def split_two(value):
    high = value.astype(jnp.bfloat16)
    low = (value - high.astype(np.float64)).astype(jnp.bfloat16)
    return high, low


def constants():
    first = tile_channel()
    position = np.arange(HALF)
    tables, selects = [], []
    for which in range(2):
        order = first + which + 1
        phase = (order[:, None] * position[None, :]) % POINTS
        angle = phase * (2.0 * math.pi / POINTS)
        both = np.concatenate([np.cos(angle), -np.sin(angle)]) / math.sqrt(POINTS)
        tables.append(np.concatenate(split_two(both)))
        pick = (first + which)[:, None] == np.arange(CHANNELS)[None, :]
        selects.append(np.concatenate([pick, pick]))
    lane = np.arange(4 * LANES)
    device, rest = np.divmod(lane, LANES)
    spectrum, within = np.divmod(rest, IN_DEV)
    target = spectrum * LANES + device * IN_DEV + within
    permute = np.zeros((4 * LANES, 4 * LANES))
    permute[lane, target] = 1.0
    return (
        np.stack(tables).astype(jnp.bfloat16),
        np.stack(selects).astype(jnp.bfloat16),
        permute.astype(jnp.bfloat16),
    )


def transposed_dot(left, right):
    return lax.dot_general(left, right, (((1,), (1,)), ((), ())), preferred_element_type=F32)


def gather_kernel(
    volt_ref, taper_ref, gain_ref, table_hbm, select_ref, permute_hbm, out_ref,
    volts, table, permute, sums, halo_sums, stage, halo_out, halo_in, tiles, other, gathered,
    load_sem, const_sem, halo_sem, swap_send, swap_recv, ring_send, ring_recv,
):
    chan, feed = lax.axis_index("chan"), lax.axis_index("feed")
    core = chan % 2
    parity = (chan // 2) % 2
    column = chan // 4
    high = 2 * feed + parity
    place = column * 2 + core

    def at(where, level):
        level = (level + RING) % RING
        return {"chan": (where // 2) * 4 + (level % 2) * 2 + where % 2, "feed": level // 2}

    def load(half):
        rows = pl.ds(8 * half, 8)
        for index in range(POINTS // LANES):
            source = volt_ref.at[:, rows, pl.ds(index * LANES, LANES)]
            pltpu.make_async_copy(source, volts.at[index, :, rows], load_sem.at[half]).start()

    def loaded(half):
        target = volts.at[:, :, pl.ds(8 * half, 8)]
        pltpu.make_async_copy(target, target, load_sem.at[half]).wait()

    for half in (1, 0):
        load(half)
        if half == 1:
            table_copy = pltpu.make_async_copy(table_hbm, table, const_sem.at[0])
            table_copy.start()
    permute_copy = pltpu.make_async_copy(permute_hbm, permute, const_sem.at[1])
    permute_copy.start()

    barrier = pltpu.get_barrier_semaphore()

    def greet(step, _):
        pl.semaphore_signal(
            barrier, inc=1, device_id=at((place + step) % SOURCES, high), device_id_type=MESH
        )
        return 0

    lax.fori_loop(1, SOURCES, greet, 0)
    for hop in (-2, -1, 1, 2):
        pl.semaphore_signal(barrier, inc=1, device_id=at(place, high + hop), device_id_type=MESH)

    flat = volts.reshape(POINTS // LANES, IN_DEV * SPECS, LANES)

    def block(index, spectrum, step):
        rows = pl.ds(index * 16 * SPECS + spectrum, 16, stride=SPECS)
        return flat[step, rows, :].astype(F32)

    def keep(target, row, lanes, first, second):
        for which, value in enumerate((first - second, first + second)):
            upper = value.astype(BF16)
            lower = (value - upper.astype(F32)).astype(BF16)
            target[which, 0, row, lanes] = upper
            target[which, 1, row, lanes] = lower

    def tapers(lanes):
        return [taper_ref[tap : tap + 1, lanes] for tap in range(TAPS)]

    def lanes_of(step):
        start = pl.multiple_of(step * LANES, LANES)
        return pl.ds(start, LANES), pl.ds(start + HALF, LANES)

    def halo_step(step, _):
        index = step % 2
        here, beyond = lanes_of(step // 2)
        pair = []
        for lanes, tile in ((here, step // 2), (beyond, step // 2 + HALF // LANES)):
            taps = tapers(lanes)
            held = [block(index, SPECS - 3 + back, tile) for back in range(3)]
            pair.append(
                [sum(taps[tap] * held[row + tap] for tap in range(3 - row)) for row in range(3)]
            )
        for row in range(3):
            start = pl.multiple_of(row * IN_DEV + index * 16, 16)
            keep(halo_sums, pl.ds(start, 16), here, pair[0][row], pair[1][row])
        return 0

    def main_step(step, _):
        index = step % 2
        here, beyond = lanes_of(step // 2)
        first_taps, second_taps = tapers(here), tapers(beyond)
        first, second = [], []
        for row in range(SPECS):
            first.append(block(index, row, step // 2))
            second.append(block(index, row, step // 2 + HALF // LANES))
            reach = [tap for tap in range(TAPS) if row - 3 + tap >= 0]
            one = sum(first_taps[tap] * first[row - 3 + tap] for tap in reach)
            two = sum(second_taps[tap] * second[row - 3 + tap] for tap in reach)
            start = pl.multiple_of(row * IN_DEV + index * 16, 16)
            keep(sums, pl.ds(start, 16), here, one, two)
        return 0

    def transform(source, which, rows):
        wide = transposed_dot(table[which], source[which, 0, rows])
        narrow = transposed_dot(table[which, :LANES], source[which, 1, rows])
        return wide[:LANES] + wide[LANES:] + narrow

    halo_sums[:, :, 3 * IN_DEV :] = jnp.zeros((2, 2, IN_DEV, HALF), BF16)
    loaded(1)
    lax.fori_loop(0, 2 * HALF // LANES, halo_step, 0)
    table_copy.wait()
    for which in range(2):
        halo_out[which] = transform(halo_sums, which, pl.ds(0, LANES)).astype(BF16)

    pl.semaphore_wait(barrier, SOURCES - 1 + 4)
    halo_copy = pltpu.make_async_remote_copy(
        src_ref=halo_out, dst_ref=halo_in, send_sem=halo_sem.at[0], recv_sem=halo_sem.at[1],
        device_id=at(place, high + 2), device_id_type=MESH,
    )

    @pl.when(feed < RING // 2 - 1)
    def _():
        halo_copy.start()

    loaded(0)
    lax.fori_loop(0, 2 * HALF // LANES, main_step, 0)

    gain_rows = jnp.concatenate([gain_ref[...].astype(F32).astype(BF16)] * 4, axis=0)

    @pl.when(feed == 0)
    def _():
        halo_in[...] = jnp.zeros_like(halo_in)

    @pl.when(feed > 0)
    def _():
        halo_copy.wait_recv()

    for which in range(2):
        factor = transposed_dot(select_ref[which], gain_rows) * (1.0 / 4096.0)
        for part in range(2):
            lines = pl.ds(part * 2 * LANES, 2 * LANES)
            spectra = transform(sums, which, lines)
            for within in range(2):
                group = part * 2 + within
                value = spectra[:, within * LANES : (within + 1) * LANES]
                if group == 0:
                    value = value + halo_in[which].astype(F32)
                value = value * factor
                for side in range(2):
                    rows = pl.ds(side * 8 + which * 4 + group, 2 * SOURCES, stride=TILE)
                    stage[rows, :] = value[side * 2 * SOURCES : (side + 1) * 2 * SOURCES]
    tiles[...] = stage[...].astype(BF16).reshape(2, SOURCES, TILE, LANES)

    def swap(step, kind, start):
        to = (place + step) % SOURCES
        source = tiles.at[(parity + 1 + kind) % 2, to]
        target = gathered.at[high, place] if kind else other.at[place]
        copy = pltpu.make_async_remote_copy(
            src_ref=source, dst_ref=target, send_sem=swap_send.at[kind], recv_sem=swap_recv.at[kind],
            device_id=at(to, high), device_id_type=MESH,
        )
        copy.start()

    for kind in range(2):

        def swap_step(step, _, kind=kind):
            swap(step, kind, True)
            return 0

        lax.fori_loop(1, SOURCES, swap_step, 0)
        source = tiles.at[(parity + 1 + kind) % 2, place]
        target = gathered.at[high, place] if kind else other.at[place]
        pltpu.make_async_copy(source, target, swap_recv.at[kind]).start()

    def landed(kind):
        whole = gathered.at[high] if kind else other
        pltpu.make_async_copy(whole, whole, swap_recv.at[kind]).wait()

    def ring(slot, chunk):
        up = slot % 2 == 0
        sign = 1 if up else -1
        piece = pl.ds(chunk * PIECE, PIECE)
        kind = slot // 2
        if kind == 0:
            source, origin, hop = other.at[piece], high, sign
        elif kind == 1:
            source, origin, hop = gathered.at[high, piece], high, 2 * sign
        elif kind == 2:
            origin, hop = (high - sign + RING) % RING, 2 * sign
            source = gathered.at[origin, piece]
        else:
            origin, hop = (high - 2 * sign + RING) % RING, 2 * sign
            source = gathered.at[origin, piece]
        return pltpu.make_async_remote_copy(
            src_ref=source, dst_ref=gathered.at[origin, piece],
            send_sem=ring_send.at[slot, chunk], recv_sem=ring_recv.at[slot, chunk],
            device_id=at(place, high + hop), device_id_type=MESH,
        )

    def arrival(slot, chunk):
        sign = 1 if slot % 2 == 0 else -1
        reach = {0: 1, 1: 2, 2: 3, 3: 4}[slot // 2]
        origin = (high - reach * sign + RING) % RING
        target = gathered.at[origin, pl.ds(chunk * PIECE, PIECE)]
        pltpu.make_async_remote_copy(
            src_ref=target, dst_ref=target,
            send_sem=ring_send.at[slot, chunk], recv_sem=ring_recv.at[slot, chunk],
            device_id=at(place, high + 1), device_id_type=MESH,
        ).wait_recv()

    half_chunks = (range(CHUNKS // 2), range(CHUNKS // 2, CHUNKS))
    sent = []

    def send(slot, chunk):
        copy = ring(slot, chunk)
        copy.start()
        sent.append(copy)

    landed(0)
    for chunk in range(CHUNKS):
        send(0, chunk)
        send(1, chunk)
    landed(1)
    for chunk in range(CHUNKS):
        send(2, chunk)
        send(3, chunk)
    for chunk in range(CHUNKS):
        for slot in (0, 1):
            arrival(slot, chunk)
            send(slot + 4, chunk)
    for step in range(CHUNKS):
        for slot in (2, 3):
            arrival(slot, step)
            if step in half_chunks[slot - 2]:
                send(slot + 4, step)
    for chunk in range(CHUNKS):
        for slot in (4, 5):
            arrival(slot, chunk)
    for slot in (6, 7):
        for chunk in half_chunks[slot - 6]:
            arrival(slot, chunk)

    permute_copy.wait()
    for shard in range(RING // 2):
        turned = None
        for side in range(4):
            low, device = divmod(side, 2)
            held = gathered[2 * shard + low].reshape(COLUMNS, 2, TILE, LANES)[:, device]
            term = jnp.dot(
                held.reshape(COLUMNS * TILE, LANES), permute[side * LANES : (side + 1) * LANES],
                preferred_element_type=F32,
            )
            turned = term if turned is None else turned + term
        turned = turned.astype(BF16)
        for spectrum in range(4):
            for where in range(COLUMNS):
                row = (shard * 4 + spectrum) * TILE
                out_ref[row : row + TILE, where * LANES : (where + 1) * LANES] = turned[
                    where * TILE : (where + 1) * TILE, spectrum * LANES : (spectrum + 1) * LANES
                ]

    for kind in range(2):
        some = tiles.at[0, pl.ds(0, SOURCES - 1)]
        pltpu.make_async_copy(some, some, swap_send.at[kind]).wait()
    for copy in sent:
        copy.wait_send()

    @pl.when(feed < RING // 2 - 1)
    def _():
        halo_copy.wait_send()


def correlate_kernel(signal_ref, out_ref, left):
    feed = lax.axis_index("feed")
    rows = out_ref.shape[2]
    depth = signal_ref.shape[0]

    @pl.when(pl.program_id(0) == 0)
    def _():
        own = signal_ref[:, pl.ds(pl.multiple_of(feed * rows, rows), rows)].astype(F32)
        own = own.reshape(depth // TILE, 2, 8, rows)
        swapped = jnp.stack([own[:, 1], -own[:, 0]], axis=1)
        second = lax.broadcasted_iota(jnp.int32, own.shape, 2) >= 4
        for which in range(2):
            for part, value in enumerate((own, swapped)):
                masked = jnp.where(second if which else ~second, value, 0.0)
                left[which, part] = masked.reshape(depth, rows).T.astype(BF16)

    columns = out_ref.shape[3]
    start = pl.multiple_of(pl.program_id(0) * columns, columns)
    right = signal_ref[:, pl.ds(start, columns)]
    for which in range(2):
        for part in range(2):
            summed = jnp.dot(left[which, part], right, preferred_element_type=F32)
            out_ref[which, part] = (summed * (1.0 / 64.0)).astype(BF16)


def on_device(voltages, taper, gains):
    table, select, permute = (jnp.asarray(value) for value in constants())
    inputs = SOURCES * 2 * IN_DEV
    depth = 4 * 4 * TILE
    whole = pl.BlockSpec(memory_space=pltpu.VMEM)
    anywhere = pl.BlockSpec(memory_space=pl.ANY)
    signals = pl.pallas_call(
        gather_kernel,
        out_shape=jax.ShapeDtypeStruct((depth, inputs), BF16),
        in_specs=[anywhere, whole, whole, anywhere, whole, anywhere],
        out_specs=whole,
        scratch_shapes=[
            pltpu.VMEM((POINTS // LANES, IN_DEV, SPECS, LANES), jnp.int32),
            pltpu.VMEM(table.shape, BF16),
            pltpu.VMEM(permute.shape, BF16),
            pltpu.VMEM((2, 2, SPECS * IN_DEV, HALF), BF16),
            pltpu.VMEM((2, 2, LANES, HALF), BF16),
            pltpu.VMEM((2 * SOURCES * TILE, LANES), F32),
            pltpu.VMEM((2, LANES, LANES), BF16),
            pltpu.VMEM((2, LANES, LANES), BF16),
            pltpu.VMEM((2, SOURCES, TILE, LANES), BF16),
            pltpu.VMEM((SOURCES, TILE, LANES), BF16),
            pltpu.VMEM((RING, SOURCES, TILE, LANES), BF16),
            pltpu.SemaphoreType.DMA((2,)),
            pltpu.SemaphoreType.DMA((2,)),
            pltpu.SemaphoreType.DMA((2,)),
            pltpu.SemaphoreType.DMA((2,)),
            pltpu.SemaphoreType.DMA((2,)),
            pltpu.SemaphoreType.DMA((8, CHUNKS)),
            pltpu.SemaphoreType.DMA((8, CHUNKS)),
        ],
        compiler_params=pltpu.CompilerParams(
            collective_id=0, has_side_effects=True, vmem_limit_bytes=48 * 1024 * 1024
        ),
    )(voltages, taper, gains, table, select, permute)
    rows, columns = inputs // 4, 256
    return pl.pallas_call(
        correlate_kernel,
        grid=(inputs // columns,),
        out_shape=jax.ShapeDtypeStruct((2, 2, rows, inputs), BF16),
        in_specs=[pl.BlockSpec((depth, inputs), lambda step: (0, 0))],
        out_specs=pl.BlockSpec((2, 2, rows, columns), lambda step: (0, 0, 0, step)),
        scratch_shapes=[pltpu.VMEM((2, 2, rows, depth), BF16)],
        compiler_params=pltpu.CompilerParams(vmem_limit_bytes=48 * 1024 * 1024),
    )(signals)


def solution(mesh):
    placed = (P("chan", "feed", None), P(), P("chan", None))
    return jax.shard_map(
        on_device,
        mesh=mesh,
        in_specs=placed,
        out_specs=P("chan", None, "feed", None),
        check_vma=False,
    )
```

time: 141 us -> 54.9 us (0.39)
  the two profiles are of different devices: /device:TPU:1 before, /device:TPU:8 now
where the time goes in v1:
time: 54.9 us; the launch traced here: 54.5 us
  Pallas kernels  49.9 us (91%)
  local copies, waits for them, and re-layouts  4.58 us (8%)
    pallas_call x1, Pallas kernels, on_device(): pl.pallas_call(gather_kernel, out_shape=jax.ShapeDtypeStruct((depth, inpu...  43.4 us
    pallas_call x1, Pallas kernels, on_device(): pl.pallas_call(correlate_kernel, grid=(inputs // columns,), out_shape=jax...  6.49 us
    unnamed x10, local copies, waits for them, and re-layouts  4.58 us

profile of v1, /device:TPU:8, one launch (start us, length us, event | category | flops | bytes accessed | tf_op | source)
XLA Modules:
  0.0 54.5 jit_solution(17145334046998719403)
XLA Ops:
  0.0 0.0 copy-start
  0.0 1.2 %copy-done = bf16[2,256,1024]{2,1,0:T(8,128)(2,1)S(1)} copy-done((bf16[2,256,1024]{2,1,0:T(8,128)(2,1)S(1)}, bf16[2,256,1024]{2,1,0:T(8,128)(2,1)}, u32[]{:S(2)}) %copy-start) | copy-done | bytes 1048600
  1.2 0.0 copy-start.1
  1.2 1.0 %copy-done.1 = bf16[512,512]{1,0:T(8,128)(2,1)S(1)} copy-done((bf16[512,512]{1,0:T(8,128)(2,1)S(1)}, bf16[512,512]{1,0:T(8,128)(2,1)}, u32[]{:S(2)}) %copy-start.1) | copy-done | bytes 524312
  2.3 0.0 copy-start.2
  2.3 0.8 %copy-done.2 = bf16[2,128,128]{2,1,0:T(8,128)(2,1)S(1)} copy-done((bf16[2,128,128]{2,1,0:T(8,128)(2,1)S(1)}, bf16[2,128,128]{2,1,0:T(8,128)(2,1)}, u32[]{:S(2)}) %copy-start.2) | copy-done | bytes 65560
  3.1 0.0 copy-start.3
  3.1 0.8 %copy-done.3 = f32[4,2048]{1,0:T(4,128)S(1)} copy-done((f32[4,2048]{1,0:T(4,128)S(1)}, f32[4,2048]{1,0:T(4,128)}, u32[]{:S(2)}) %copy-start.3) | copy-done | bytes 32792
  3.9 0.0 copy-start.4
  3.9 0.7 %copy-done.4 = s32[32,128]{1,0:T(8,128)S(1)} copy-done((s32[32,128]{1,0:T(8,128)S(1)}, s32[32,128]{1,0:T(8,128)}, u32[]{:S(2)}) %copy-start.4) | copy-done | bytes 16408
  4.6 43.4 %shard_map.64.signal_ref = bf16[256,2048]{1,0:T(8,128)(2,1)S(1)} custom-call(s32[32,16,2048]{2,1,0:T(8,128)} %volt_ref.1, f32[4,2048]{1,0:T(4,128)S(1)} %copy-done.3, s32[32,128]{1,0:T(8,128)S(1)} %copy-done.4, bf16[2,256,1024]{2,1,0:T(8,128)(2,1)S(1)} %copy-done, bf16[2,128,128]{2,1,0:T(8,128)(2,1)S(1)} %copy-done.2, bf16[512,512]{1,0:T(8,128)(2,1)S(1)} %copy-done.1), custom_call_target="tpu_custom_call" | custom-call | tf_op jit(solution)/shard_map/pallas_call | solution.py:368
  48.0 6.5 %shard_map.65 = bf16[2,2,512,2048]{3,2,1,0:T(8,128)(2,1)} custom-call(bf16[256,2048]{1,0:T(8,128)(2,1)S(1)} %shard_map.64.signal_ref), custom_call_target="tpu_custom_call" | custom-call | tf_op jit(solution)/shard_map/pallas_call | solution.py:398
Async XLA Ops:
  0.0 1.2 %copy-start = (bf16[2,256,1024]{2,1,0:T(8,128)(2,1)S(1)}, bf16[2,256,1024]{2,1,0:T(8,128)(2,1)}, u32[]{:S(2)}) copy-start(bf16[2,256,1024]{2,1,0:T(8,128)(2,1)} %constant.6.clone.table_hbm) | copy-start | bytes 3145732
  1.2 1.0 %copy-start.1 = (bf16[512,512]{1,0:T(8,128)(2,1)S(1)}, bf16[512,512]{1,0:T(8,128)(2,1)}, u32[]{:S(2)}) copy-start(bf16[512,512]{1,0:T(8,128)(2,1)} %constant.8.clone.permute_hbm) | copy-start | bytes 1572868
  2.3 0.8 %copy-start.2 = (bf16[2,128,128]{2,1,0:T(8,128)(2,1)S(1)}, bf16[2,128,128]{2,1,0:T(8,128)(2,1)}, u32[]{:S(2)}) copy-start(bf16[2,128,128]{2,1,0:T(8,128)(2,1)} %constant.7.clone.select_ref) | copy-start | bytes 196612
  3.1 0.8 %copy-start.3 = (f32[4,2048]{1,0:T(4,128)S(1)}, f32[4,2048]{1,0:T(4,128)}, u32[]{:S(2)}) copy-start(f32[4,2048]{1,0:T(4,128)} %taper_ref.1) | copy-start | bytes 98308
  3.9 0.7 %copy-start.4 = (s32[32,128]{1,0:T(8,128)S(1)}, s32[32,128]{1,0:T(8,128)}, u32[]{:S(2)}) copy-start(s32[32,128]{1,0:T(8,128)} %gain_ref.1) | copy-start | bytes 49156

commit v2 on v1

v2 whole, which is shorter than its diff:
```python
import functools
import math

import jax
import jax.numpy as jnp
import numpy as np
from jax import lax
from jax.experimental import pallas as pl
from jax.experimental.pallas import tpu as pltpu
from jax.sharding import PartitionSpec as P

MESH = pl.DeviceIdType.MESH
F32, BF16 = jnp.float32, jnp.bfloat16

POINTS = 2048
HALF = POINTS // 2
CHANNELS = 128
IN_DEV = 32
SPECS = 16
TAPS = 4
COLUMNS = 16
RING = 8
SOURCES = 2 * COLUMNS
TILE = 16
LANES = 128
CHUNKS = 2
PIECE = SOURCES // CHUNKS


def tile_channel():
    parity, place = np.divmod(np.arange(2 * SOURCES), SOURCES)
    column, core = np.divmod(place, 2)
    return 2 * (column * 4 + parity * 2 + core)


def split_two(value):
    high = value.astype(jnp.bfloat16)
    low = (value - high.astype(np.float64)).astype(jnp.bfloat16)
    return high, low


def constants():
    first = tile_channel()
    position = np.arange(HALF)
    tables, selects = [], []
    for which in range(2):
        order = first + which + 1
        phase = (order[:, None] * position[None, :]) % POINTS
        angle = phase * (2.0 * math.pi / POINTS)
        both = np.concatenate([np.cos(angle), -np.sin(angle)]) / math.sqrt(POINTS)
        tables.append(np.concatenate(split_two(both)))
        pick = (first + which)[:, None] == np.arange(CHANNELS)[None, :]
        selects.append(np.concatenate([pick, pick]))
    lane = np.arange(4 * LANES)
    device, rest = np.divmod(lane, LANES)
    spectrum, within = np.divmod(rest, IN_DEV)
    target = spectrum * LANES + device * IN_DEV + within
    permute = np.zeros((4 * LANES, 4 * LANES))
    permute[lane, target] = 1.0
    line = np.arange(LANES)
    within = line % TILE
    turns = []
    for which in range(2):
        chosen = (within // 4) % 2 == which
        same = np.diag(np.where(chosen, 1.0 / 64.0, 0.0))
        cross = np.zeros((LANES, LANES))
        cross[line, line ^ 8] = np.where(within < 8, -1.0 / 64.0, 1.0 / 64.0)
        turns += [same, cross * chosen[None, :]]
    return (
        np.stack(tables).astype(jnp.bfloat16),
        np.stack(selects).astype(jnp.bfloat16),
        permute.astype(jnp.bfloat16),
        np.concatenate(turns, axis=1).astype(jnp.bfloat16),
    )


def transposed_dot(left, right):
    return lax.dot_general(left, right, (((1,), (1,)), ((), ())), preferred_element_type=F32)


def gather_kernel(
    volt_hbm, taper_hbm, gain_hbm, table_hbm, select_hbm, permute_hbm, turns_hbm, out_ref, left_ref,
    volts, taper_ref, gain_ref, table, select_ref, permute, turns, sums, halo_sums, stage, halo_out, halo_in, tiles, other, gathered,
    load_sem, const_sem, halo_sem, swap_send, swap_recv, ring_send, ring_recv,
):
    chan, feed = lax.axis_index("chan"), lax.axis_index("feed")
    core = lax.rem(chan, 2)
    parity = lax.rem(lax.div(chan, 2), 2)
    column = lax.div(chan, 4)
    high = 2 * feed + parity
    place = column * 2 + core

    def level_of(level):
        return lax.rem(level + RING, RING)

    def ring_at(hop):
        level = level_of(high + hop)
        return {"chan": column * 4 + lax.rem(level, 2) * 2 + core, "feed": lax.div(level, 2)}

    def plane_at(where):
        return {"chan": lax.div(where, 2) * 4 + parity * 2 + lax.rem(where, 2)}

    def load(half, part):
        some = pl.ds(part * IN_DEV // 2, IN_DEV // 2)
        return pltpu.make_async_copy(
            volt_hbm.at[some, half], volts.at[some, half], load_sem.at[half, part]
        )

    small = (
        (taper_hbm, taper_ref), (table_hbm, table), (gain_hbm, gain_ref), (select_hbm, select_ref),
        (permute_hbm, permute), (turns_hbm, turns),
    )
    copies = [pltpu.make_async_copy(*pair, const_sem.at[n]) for n, pair in enumerate(small)]
    taper_copy, table_copy, gain_copy, select_copy, permute_copy, turns_copy = copies
    taper_copy.start()
    for half in (1, 0):
        for part in range(2):
            load(half, part).start()
        if half == 1:
            table_copy.start()
    for copy in copies[2:]:
        copy.start()

    barrier = pltpu.get_barrier_semaphore()

    def greet(step, _):
        pl.semaphore_signal(
            barrier, inc=1, device_id=plane_at(lax.rem(place + step, SOURCES)), device_id_type=MESH
        )
        return 0

    lax.fori_loop(1, SOURCES, greet, 0)
    for hop in (-2, -1, 1, 2):
        pl.semaphore_signal(barrier, inc=1, device_id=ring_at(hop), device_id_type=MESH)

    flat = volts.reshape(IN_DEV * SPECS * POINTS // LANES, LANES)

    def block(part, spectrum, tile):
        half, line = divmod(spectrum, 8)
        start = (part * IN_DEV + half) * POINTS // LANES * 8 + tile * 8 + line
        return flat[pl.ds(start, 16, stride=SPECS * POINTS // LANES), :].astype(F32)

    def keep(target, row, lanes, first, second):
        for which, value in enumerate((first - second, first + second)):
            upper = value.astype(BF16)
            lower = (value - upper.astype(F32)).astype(BF16)
            target[which, 0, row, lanes] = upper
            target[which, 1, row, lanes] = lower

    def tapers(lanes):
        return [taper_ref[tap : tap + 1, lanes] for tap in range(TAPS)]

    def lanes_of(step):
        start = pl.multiple_of(step * LANES, LANES)
        return pl.ds(start, LANES), pl.ds(start + HALF, LANES)

    def halo_step(step, _, part):
        here, beyond = lanes_of(step)
        pair = []
        for lanes, tile in ((here, step), (beyond, step + HALF // LANES)):
            taps = tapers(lanes)
            held = [block(part, SPECS - 3 + back, tile) for back in range(3)]
            pair.append(
                [sum(taps[tap] * held[row + tap] for tap in range(3 - row)) for row in range(3)]
            )
        for row in range(3):
            keep(halo_sums, pl.ds(row * IN_DEV + part * 16, 16), here, pair[0][row], pair[1][row])
        return 0

    def main_step(step, _, part):
        here, beyond = lanes_of(step)
        first_taps, second_taps = tapers(here), tapers(beyond)
        first, second = [], []
        for row in range(SPECS):
            first.append(block(part, row, step))
            second.append(block(part, row, step + HALF // LANES))
            reach = [tap for tap in range(TAPS) if row - 3 + tap >= 0]
            one = sum(first_taps[tap] * first[row - 3 + tap] for tap in reach)
            two = sum(second_taps[tap] * second[row - 3 + tap] for tap in reach)
            keep(sums, pl.ds(row * IN_DEV + part * 16, 16), here, one, two)
        return 0

    def transform(source, which, rows):
        wide = transposed_dot(table[which], source[which, 0, rows])
        narrow = transposed_dot(table[which, :LANES], source[which, 1, rows])
        return wide[:LANES] + wide[LANES:] + narrow

    halo_sums[:, :, 3 * IN_DEV :] = jnp.zeros((2, 2, IN_DEV, HALF), BF16)
    taper_copy.wait()
    for part in range(2):
        load(1, part).wait()
        lax.fori_loop(0, HALF // LANES, functools.partial(halo_step, part=part), 0)
    table_copy.wait()
    for which in range(2):
        halo_out[which] = transform(halo_sums, which, pl.ds(0, LANES)).astype(BF16)

    pl.semaphore_wait(barrier, SOURCES - 1 + 4)
    halo_copy = pltpu.make_async_remote_copy(
        src_ref=halo_out, dst_ref=halo_in, send_sem=halo_sem.at[0], recv_sem=halo_sem.at[1],
        device_id=ring_at(2), device_id_type=MESH,
    )

    @pl.when(feed < RING // 2 - 1)
    def _():
        halo_copy.start()

    for part in range(2):
        load(0, part).wait()
        lax.fori_loop(0, HALF // LANES, functools.partial(main_step, part=part), 0)

    gain_copy.wait()
    select_copy.wait()
    gain_rows = jnp.concatenate([gain_ref[...].astype(F32).astype(BF16)] * 4, axis=0)

    factors = [transposed_dot(select_ref[which], gain_rows) * (1.0 / 4096.0) for which in range(2)]

    def settle(which, group, value):
        value = value * factors[which]
        for side in range(2):
            rows = pl.ds(side * 8 + which * 4 + group, 2 * SOURCES, stride=TILE)
            stage[rows, :] = value[side * 2 * SOURCES : (side + 1) * 2 * SOURCES]

    firsts = []
    for which in range(2):
        for part in (1, 0):
            spectra = transform(sums, which, pl.ds(part * 2 * LANES, 2 * LANES))
            for within in range(2):
                value = spectra[:, within * LANES : (within + 1) * LANES]
                if part + within == 0:
                    firsts.append(value)
                else:
                    settle(which, part * 2 + within, value)

    @pl.when(feed == 0)
    def _():
        halo_in[...] = jnp.zeros_like(halo_in)

    @pl.when(feed > 0)
    def _():
        halo_copy.wait_recv()

    for which in range(2):
        settle(which, 0, firsts[which] + halo_in[which].astype(F32))
    tiles[...] = stage[...].astype(BF16).reshape(2, SOURCES, TILE, LANES)

    def swap(step, kind, start):
        to = lax.rem(place + step, SOURCES)
        source = tiles.at[lax.rem(parity + 1 + kind, 2), to]
        target = gathered.at[high, place] if kind else other.at[place]
        copy = pltpu.make_async_remote_copy(
            src_ref=source, dst_ref=target, send_sem=swap_send.at[kind], recv_sem=swap_recv.at[kind],
            device_id=plane_at(to), device_id_type=MESH,
        )
        copy.start()

    for kind in range(2):

        def swap_step(step, _, kind=kind):
            swap(step, kind, True)
            return 0

        lax.fori_loop(1, SOURCES, swap_step, 0)
        source = tiles.at[lax.rem(parity + 1 + kind, 2), place]
        target = gathered.at[high, place] if kind else other.at[place]
        pltpu.make_async_copy(source, target, swap_recv.at[kind]).start()

    def landed(kind):
        whole = gathered.at[high] if kind else other
        pltpu.make_async_copy(whole, whole, swap_recv.at[kind]).wait()

    def ring(slot, chunk):
        up = slot % 2 == 0
        sign = 1 if up else -1
        piece = pl.ds(chunk * PIECE, PIECE)
        kind = slot // 2
        if kind == 0:
            source, origin, hop = other.at[piece], high, sign
        elif kind == 1:
            source, origin, hop = gathered.at[high, piece], high, 2 * sign
        elif kind == 2:
            origin, hop = level_of(high - sign), 2 * sign
            source = gathered.at[origin, piece]
        else:
            origin, hop = level_of(high - 2 * sign), 2 * sign
            source = gathered.at[origin, piece]
        return pltpu.make_async_remote_copy(
            src_ref=source, dst_ref=gathered.at[origin, piece],
            send_sem=ring_send.at[slot, chunk], recv_sem=ring_recv.at[slot, chunk],
            device_id=ring_at(hop), device_id_type=MESH,
        )

    def arrival(slot, chunk):
        sign = 1 if slot % 2 == 0 else -1
        reach = {0: 1, 1: 2, 2: 3, 3: 4}[slot // 2]
        origin = level_of(high - reach * sign)
        target = gathered.at[origin, pl.ds(chunk * PIECE, PIECE)]
        pltpu.make_async_remote_copy(
            src_ref=target, dst_ref=target,
            send_sem=ring_send.at[slot, chunk], recv_sem=ring_recv.at[slot, chunk],
            device_id=ring_at(1), device_id_type=MESH,
        ).wait_recv()

    half_chunks = (range(CHUNKS // 2), range(CHUNKS // 2, CHUNKS))
    sent = []

    def send(slot, chunk):
        copy = ring(slot, chunk)
        copy.start()
        sent.append(copy)

    def order(slot, step):
        return step if slot != 3 else CHUNKS - 1 - step

    landed(0)
    send(0, 0)
    send(1, 0)
    landed(1)
    for step in range(CHUNKS):
        for slot in range(4):
            if step or slot >= 2:
                send(slot, order(slot, step))
    for step in range(CHUNKS):
        for slot in range(4):
            chunk = order(slot, step)
            arrival(slot, chunk)
            if slot < 2 or chunk in half_chunks[slot - 2]:
                send(slot + 4, chunk)

    permute_copy.wait()
    turns_copy.wait()

    def turn(order, shard):
        shard = lax.rem(shard + 4, 4)
        turned = None
        for side in range(4):
            low, device = divmod(side, 2)
            held = gathered[2 * shard + low].reshape(COLUMNS, 2, TILE, LANES)[:, device]
            term = jnp.dot(
                held.reshape(COLUMNS * TILE, LANES), permute[side * LANES : (side + 1) * LANES],
                preferred_element_type=F32,
            )
            turned = term if turned is None else turned + term
        turned = turned.astype(BF16)
        for spectrum in range(4):
            for where in range(COLUMNS):
                row = (order * 4 + spectrum) * TILE
                out_ref[row : row + TILE, where * LANES : (where + 1) * LANES] = turned[
                    where * TILE : (where + 1) * TILE, spectrum * LANES : (spectrum + 1) * LANES
                ]

    def prepare(pair):
        rows = left_ref.shape[1]
        own = out_ref[pair * LANES : (pair + 1) * LANES, pl.ds(pl.multiple_of(feed * rows, rows), rows)]
        moved = jnp.dot(own.T, turns[...], preferred_element_type=F32).astype(BF16)
        for index in range(4):
            left_ref[index, :, pair * LANES : (pair + 1) * LANES] = moved[
                :, index * LANES : (index + 1) * LANES
            ]

    turn(0, feed)
    turn(1, feed - 1 + 2 * parity)
    prepare(0)
    for chunk in range(CHUNKS):
        for slot in (4, 5):
            arrival(slot, chunk)
    turn(2, feed + 1 - 2 * parity)
    for slot in (6, 7):
        for chunk in half_chunks[slot - 6]:
            arrival(slot, chunk)
    turn(3, feed + 2)
    prepare(1)
    for kind in range(2):
        some = tiles.at[0, pl.ds(0, SOURCES - 1)]
        pltpu.make_async_copy(some, some, swap_send.at[kind]).wait()
    for copy in sent:
        copy.wait_send()

    @pl.when(feed < RING // 2 - 1)
    def _():
        halo_copy.wait_send()


def correlate_kernel(signal_ref, left_ref, out_hbm, whole, sem):
    columns = 512
    count = whole.shape[3] // columns
    copies = []
    for index in range(4 * count):
        which, part, block = index // (2 * count), index // count % 2, index % count
        some = pl.ds(block * columns, columns)
        summed = jnp.dot(left_ref[2 * which + part], signal_ref[:, some], preferred_element_type=F32)
        whole[which, part, :, some] = summed.astype(BF16)
        copy = pltpu.make_async_copy(
            whole.at[which, part, :, some], out_hbm.at[which, part, :, some], sem.at[index]
        )
        copy.start()
        copies.append(copy)
    for copy in copies:
        copy.wait()


def on_device(voltages, taper, gains):
    table, select, permute, turns = (jnp.asarray(value) for value in constants())
    laid = voltages.reshape(IN_DEV, 2, 8, POINTS // LANES, LANES).transpose(0, 1, 3, 2, 4)
    operands = (laid, taper, gains, table, select, permute, turns)
    inputs = SOURCES * 2 * IN_DEV
    rows = inputs // 4
    depth = 4 * 4 * TILE
    whole = pl.BlockSpec(memory_space=pltpu.VMEM)
    signals, left = pl.pallas_call(
        gather_kernel,
        out_shape=(
            jax.ShapeDtypeStruct((depth, inputs), BF16),
            jax.ShapeDtypeStruct((4, rows, depth), BF16),
        ),
        in_specs=[pl.BlockSpec(memory_space=pl.ANY)] * len(operands),
        out_specs=(whole, whole),
        scratch_shapes=[
            pltpu.VMEM(laid.shape, jnp.int32),
            pltpu.VMEM(taper.shape, F32),
            pltpu.VMEM(gains.shape, jnp.int32),
            pltpu.VMEM(table.shape, BF16),
            pltpu.VMEM(select.shape, BF16),
            pltpu.VMEM(permute.shape, BF16),
            pltpu.VMEM(turns.shape, BF16),
            pltpu.VMEM((2, 2, SPECS * IN_DEV, HALF), BF16),
            pltpu.VMEM((2, 2, LANES, HALF), BF16),
            pltpu.VMEM((2 * SOURCES * TILE, LANES), F32),
            pltpu.VMEM((2, LANES, LANES), BF16),
            pltpu.VMEM((2, LANES, LANES), BF16),
            pltpu.VMEM((2, SOURCES, TILE, LANES), BF16),
            pltpu.VMEM((SOURCES, TILE, LANES), BF16),
            pltpu.VMEM((RING, SOURCES, TILE, LANES), BF16),
            pltpu.SemaphoreType.DMA((2, 2)),
            pltpu.SemaphoreType.DMA((len(operands) - 1,)),
            pltpu.SemaphoreType.DMA((2,)),
            pltpu.SemaphoreType.DMA((2,)),
            pltpu.SemaphoreType.DMA((2,)),
            pltpu.SemaphoreType.DMA((8, CHUNKS)),
            pltpu.SemaphoreType.DMA((8, CHUNKS)),
        ],
        compiler_params=pltpu.CompilerParams(
            collective_id=0, has_side_effects=True, vmem_limit_bytes=48 * 1024 * 1024
        ),
    )(*(pltpu.with_memory_space_constraint(value, pltpu.HBM) for value in operands))
    return pl.pallas_call(
        correlate_kernel,
        out_shape=jax.ShapeDtypeStruct((2, 2, rows, inputs), BF16),
        in_specs=[whole, whole],
        out_specs=pl.BlockSpec(memory_space=pl.ANY),
        scratch_shapes=[pltpu.VMEM((2, 2, rows, inputs), BF16), pltpu.SemaphoreType.DMA((16,))],
        compiler_params=pltpu.CompilerParams(vmem_limit_bytes=32 * 1024 * 1024),
    )(signals, left)


def solution(mesh):
    placed = (P("chan", "feed", None), P(), P("chan", None))
    return jax.shard_map(
        on_device,
        mesh=mesh,
        in_specs=placed,
        out_specs=P("chan", None, "feed", None),
        check_vma=False,
    )
```

time: 54.9 us -> 45.1 us (0.82)
  the two profiles are of different devices: /device:TPU:8 before, /device:TPU:1 now
where the time goes in v2:
time: 45.1 us
  Pallas kernels  45 us (100%)
    pallas_call x1, Pallas kernels, on_device(): pl.pallas_call(gather_kernel, out_shape=(jax.ShapeDtypeStruct((depth, inp...  41.3 us
    pallas_call x1, Pallas kernels, on_device(): pl.pallas_call(correlate_kernel, out_shape=jax.ShapeDtypeStruct((2, 2, ro...  3.72 us

profile of v2, /device:TPU:1, one launch (start us, length us, event | category | flops | bytes accessed | tf_op | source)
XLA Modules:
  0.0 45.1 jit_solution(10426391212353716081)
XLA Ops:
  0.0 41.3 %shard_map.73 = (bf16[256,2048]{1,0:T(8,128)(2,1)S(1)}, bf16[4,512,256]{2,1,0:T(8,128)(2,1)S(1)}) custom-call(s32[32,2,16,8,128]{4,3,2,1,0:T(8,128)} %bitcast.3, f32[4,2048]{1,0:T(4,128)} %taper_hbm.1, s32[32,128]{1,0:T(8,128)} %gain_hbm.1, bf16[2,256,1024]{2,1,0:T(8,128)(2,1)} %constant.8.clone.table_hbm, bf16[2,128,128]{2,1,0:T(8,128)(2,1)} %constant.9.clone.select_hbm, ...), custom_call_target="tpu_custom_call" | custom-call | tf_op jit(solution)/shard_map/pallas_call | solution.py:409
  41.3 3.7 %shard_map.74 = bf16[2,2,512,2048]{3,2,1,0:T(8,128)(2,1)} custom-call(bf16[256,2048]{1,0:T(8,128)(2,1)S(1)} %get-tuple-element.7.signal_ref, bf16[4,512,256]{2,1,0:T(8,128)(2,1)S(1)} %get-tuple-element.8.left_ref), custom_call_target="tpu_custom_call" | custom-call | tf_op jit(solution)/shard_map/pallas_call | solution.py:445

commit v3 on v2

--- a/solution.py
+++ b/solution.py
@@ -23,8 +23,9 @@
 SOURCES = 2 * COLUMNS
 TILE = 16
 LANES = 128
-CHUNKS = 2
-PIECE = SOURCES // CHUNKS
+ROW = 8
+ROWS = SOURCES // ROW
+PITCH = SPECS * POINTS // LANES + 8
 
 
 def tile_channel():
@@ -80,7 +81,7 @@
 
 def gather_kernel(
     volt_hbm, taper_hbm, gain_hbm, table_hbm, select_hbm, permute_hbm, turns_hbm, out_ref, left_ref,
-    volts, taper_ref, gain_ref, table, select_ref, permute, turns, sums, halo_sums, stage, halo_out, halo_in, tiles, other, gathered,
+    volts, taper_ref, gain_ref, table, select_ref, permute, turns, sums, halo_sums, stage, halo_out, halo_in, tiles, other, passing, gathered,
     load_sem, const_sem, halo_sem, swap_send, swap_recv, ring_send, ring_recv,
 ):
     chan, feed = lax.axis_index("chan"), lax.axis_index("feed")
@@ -89,6 +90,8 @@
     column = lax.div(chan, 4)
     high = 2 * feed + parity
     place = column * 2 + core
+    line = lax.div(place, ROW)
+    near = pl.ds(pl.multiple_of(line * ROW, ROW), ROW)
 
     def level_of(level):
         return lax.rem(level + RING, RING)
@@ -102,8 +105,9 @@
 
     def load(half, part):
         some = pl.ds(part * IN_DEV // 2, IN_DEV // 2)
+        lines = pl.ds(half * POINTS // LANES * 8, POINTS // LANES * 8)
         return pltpu.make_async_copy(
-            volt_hbm.at[some, half], volts.at[some, half], load_sem.at[half, part]
+            volt_hbm.at[some, lines], volts.at[some, lines], load_sem.at[half, part]
         )
 
     small = (
@@ -133,12 +137,12 @@
     for hop in (-2, -1, 1, 2):
         pl.semaphore_signal(barrier, inc=1, device_id=ring_at(hop), device_id_type=MESH)
 
-    flat = volts.reshape(IN_DEV * SPECS * POINTS // LANES, LANES)
+    flat = volts.reshape(IN_DEV * PITCH, LANES)
 
     def block(part, spectrum, tile):
         half, line = divmod(spectrum, 8)
-        start = (part * IN_DEV + half) * POINTS // LANES * 8 + tile * 8 + line
-        return flat[pl.ds(start, 16, stride=SPECS * POINTS // LANES), :].astype(F32)
+        start = part * 16 * PITCH + half * POINTS // LANES * 8 + tile * 8 + line
+        return flat[pl.ds(start, 16, stride=PITCH), :].astype(F32)
 
     def keep(target, row, lanes, first, second):
         for which, value in enumerate((first - second, first + second)):
@@ -243,88 +247,112 @@
         settle(which, 0, firsts[which] + halo_in[which].astype(F32))
     tiles[...] = stage[...].astype(BF16).reshape(2, SOURCES, TILE, LANES)
 
-    def swap(step, kind, start):
-        to = lax.rem(place + step, SOURCES)
-        source = tiles.at[lax.rem(parity + 1 + kind, 2), to]
-        target = gathered.at[high, place] if kind else other.at[place]
-        copy = pltpu.make_async_remote_copy(
-            src_ref=source, dst_ref=target, send_sem=swap_send.at[kind], recv_sem=swap_recv.at[kind],
-            device_id=plane_at(to), device_id_type=MESH,
+    def push(source, target, send_sem, recv_sem, device):
+        return pltpu.make_async_remote_copy(
+            src_ref=source, dst_ref=target, send_sem=send_sem, recv_sem=recv_sem,
+            device_id=device, device_id_type=MESH,
         )
-        copy.start()
-
-    for kind in range(2):
-
-        def swap_step(step, _, kind=kind):
-            swap(step, kind, True)
-            return 0
-
-        lax.fori_loop(1, SOURCES, swap_step, 0)
-        source = tiles.at[lax.rem(parity + 1 + kind, 2), place]
-        target = gathered.at[high, place] if kind else other.at[place]
-        pltpu.make_async_copy(source, target, swap_recv.at[kind]).start()
-
-    def landed(kind):
-        whole = gathered.at[high] if kind else other
-        pltpu.make_async_copy(whole, whole, swap_recv.at[kind]).wait()
-
-    def ring(slot, chunk):
-        up = slot % 2 == 0
-        sign = 1 if up else -1
-        piece = pl.ds(chunk * PIECE, PIECE)
+
+    def far_row(step):
+        return lax.rem(line + step, ROWS) * ROW
+
+    def held(step, origin, start=0, count=ROW):
+        if step == 0:
+            return passing.at[origin, pl.ds(start, count)]
+        return gathered.at[origin, pl.ds(far_row(step) + start, count)]
+
+    def part_of(slot):
+        return {6: (0, ROW // 2), 7: (ROW // 2, ROW // 2)}.get(slot, (0, ROW))
+
+    def ring(slot, step):
+        sign = 1 if slot % 2 == 0 else -1
         kind = slot // 2
-        if kind == 0:
-            source, origin, hop = other.at[piece], high, sign
-        elif kind == 1:
-            source, origin, hop = gathered.at[high, piece], high, 2 * sign
-        elif kind == 2:
-            origin, hop = level_of(high - sign), 2 * sign
-            source = gathered.at[origin, piece]
+        start, count = part_of(slot)
+        hop = sign if kind == 0 else 2 * sign
+        origin = level_of(high - {0: 0, 1: 0, 2: 1, 3: 2}[kind] * sign)
+        if kind >= 2:
+            source = held(step, origin, start, count)
+        elif step == 0:
+            source = tiles.at[lax.rem(parity + 1 + kind, 2), near]
+        elif kind == 0:
+            source = other.at[pl.ds(far_row(step), ROW)]
         else:
-            origin, hop = level_of(high - 2 * sign), 2 * sign
-            source = gathered.at[origin, piece]
-        return pltpu.make_async_remote_copy(
-            src_ref=source, dst_ref=gathered.at[origin, piece],
-            send_sem=ring_send.at[slot, chunk], recv_sem=ring_recv.at[slot, chunk],
-            device_id=ring_at(hop), device_id_type=MESH,
+            source = gathered.at[high, pl.ds(far_row(step), ROW)]
+        return push(
+            source, held(step, origin, start, count),
+            ring_send.at[slot, step], ring_recv.at[slot, step], ring_at(hop),
         )
 
-    def arrival(slot, chunk):
+    def arrival(slot, step):
         sign = 1 if slot % 2 == 0 else -1
         reach = {0: 1, 1: 2, 2: 3, 3: 4}[slot // 2]
-        origin = level_of(high - reach * sign)
-        target = gathered.at[origin, pl.ds(chunk * PIECE, PIECE)]
-        pltpu.make_async_remote_copy(
-            src_ref=target, dst_ref=target,
-            send_sem=ring_send.at[slot, chunk], recv_sem=ring_recv.at[slot, chunk],
-            device_id=ring_at(1), device_id_type=MESH,
-        ).wait_recv()
-
-    half_chunks = (range(CHUNKS // 2), range(CHUNKS // 2, CHUNKS))
-    sent = []
-
-    def send(slot, chunk):
-        copy = ring(slot, chunk)
-        copy.start()
-        sent.append(copy)
-
-    def order(slot, step):
-        return step if slot != 3 else CHUNKS - 1 - step
-
-    landed(0)
-    send(0, 0)
-    send(1, 0)
-    landed(1)
-    for step in range(CHUNKS):
+        target = held(step, level_of(high - reach * sign), *part_of(slot))
+        push(target, target, ring_send.at[slot, step], ring_recv.at[slot, step], ring_at(1)).wait_recv()
+
+    def send(slot, step):
+        ring(slot, step).start()
+
+    def hand_on(step):
         for slot in range(4):
-            if step or slot >= 2:
-                send(slot, order(slot, step))
-    for step in range(CHUNKS):
-        for slot in range(4):
-            chunk = order(slot, step)
-            arrival(slot, chunk)
-            if slot < 2 or chunk in half_chunks[slot - 2]:
-                send(slot + 4, chunk)
+            arrival(slot, step)
+            send(slot + 4, step)
+
+    for slot in range(4):
+        send(slot, 0)
+
+    for kind in range(2):
+
+        def swap_step(step, _, kind=kind):
+            to = lax.rem((line + 1) * ROW + step, SOURCES)
+            source = tiles.at[lax.rem(parity + 1 + kind, 2), to]
+            target = gathered.at[high, place] if kind else other.at[place]
+            arrives = swap_recv.at[kind, ROWS - 1 - lax.div(step, ROW)]
+            push(source, target, swap_send.at[kind], arrives, plane_at(to)).start()
+            return 0
+
+        lax.fori_loop(0, SOURCES - ROW, swap_step, 0)
+
+    def landed(kind, step):
+        some = pl.ds(far_row(step), ROW)
+        whole = gathered.at[high, some] if kind else other.at[some]
+        pltpu.make_async_copy(whole, whole, swap_recv.at[kind, step]).wait()
+
+    def spread():
+        for slot in range(4, 8):
+            arrival(slot, 0)
+        own = pltpu.make_async_copy(tiles.at[parity, near], passing.at[high], swap_recv.at[0, 0])
+        own.start()
+        own.wait()
+
+        def row_step(step, _):
+            index = lax.rem(place + step, ROW)
+            push(
+                passing.at[:, index], gathered.at[:, place],
+                swap_send.at[2], swap_recv.at[1, 0], plane_at(line * ROW + index),
+            ).start()
+            return 0
+
+        lax.fori_loop(1, ROW, row_step, 0)
+        pltpu.make_async_copy(
+            passing.at[:, lax.rem(place, ROW)], gathered.at[:, place], swap_recv.at[1, 0]
+        ).start()
+
+    hand_on(0)
+    for kind in range(2):
+        for step in (1, 2):
+            landed(kind, step)
+            send(2 * kind, step)
+            send(2 * kind + 1, step)
+    spread()
+    for kind in range(2):
+        for step in (3,):
+            landed(kind, step)
+            send(2 * kind, step)
+            send(2 * kind + 1, step)
+    hand_on(1)
+    hand_on(2)
+    hand_on(3)
+    pltpu.make_async_copy(gathered.at[:, near], gathered.at[:, near], swap_recv.at[1, 0]).wait()
 
     permute_copy.wait()
     turns_copy.wait()
@@ -360,20 +388,23 @@
     turn(0, feed)
     turn(1, feed - 1 + 2 * parity)
     prepare(0)
-    for chunk in range(CHUNKS):
-        for slot in (4, 5):
-            arrival(slot, chunk)
+    for step in range(1, ROWS):
+        arrival(4, step)
+        arrival(5, step)
     turn(2, feed + 1 - 2 * parity)
-    for slot in (6, 7):
-        for chunk in half_chunks[slot - 6]:
-            arrival(slot, chunk)
+    for step in range(1, ROWS):
+        arrival(6, step)
+        arrival(7, step)
     turn(3, feed + 2)
     prepare(1)
     for kind in range(2):
-        some = tiles.at[0, pl.ds(0, SOURCES - 1)]
+        some = tiles.at[0, pl.ds(0, SOURCES - ROW)]
         pltpu.make_async_copy(some, some, swap_send.at[kind]).wait()
-    for copy in sent:
-        copy.wait_send()
+    some = passing.at[:, pl.ds(0, ROW - 1)]
+    pltpu.make_async_copy(some, some, swap_send.at[2]).wait()
+    for slot in range(8):
+        for step in range(ROWS):
+            ring(slot, step).wait_send()
 
     @pl.when(feed < RING // 2 - 1)
     def _():
@@ -401,6 +432,7 @@
 def on_device(voltages, taper, gains):
     table, select, permute, turns = (jnp.asarray(value) for value in constants())
     laid = voltages.reshape(IN_DEV, 2, 8, POINTS // LANES, LANES).transpose(0, 1, 3, 2, 4)
+    laid = laid.reshape(IN_DEV, SPECS * POINTS // LANES, LANES)
     operands = (laid, taper, gains, table, select, permute, turns)
     inputs = SOURCES * 2 * IN_DEV
     rows = inputs // 4
@@ -415,7 +447,7 @@
         in_specs=[pl.BlockSpec(memory_space=pl.ANY)] * len(operands),
         out_specs=(whole, whole),
         scratch_shapes=[
-            pltpu.VMEM(laid.shape, jnp.int32),
+            pltpu.VMEM((IN_DEV, PITCH, LANES), jnp.int32),
             pltpu.VMEM(taper.shape, F32),
             pltpu.VMEM(gains.shape, jnp.int32),
             pltpu.VMEM(table.shape, BF16),
@@ -429,14 +461,15 @@
             pltpu.VMEM((2, LANES, LANES), BF16),
             pltpu.VMEM((2, SOURCES, TILE, LANES), BF16),
             pltpu.VMEM((SOURCES, TILE, LANES), BF16),
+            pltpu.VMEM((RING, ROW, TILE, LANES), BF16),
             pltpu.VMEM((RING, SOURCES, TILE, LANES), BF16),
             pltpu.SemaphoreType.DMA((2, 2)),
             pltpu.SemaphoreType.DMA((len(operands) - 1,)),
             pltpu.SemaphoreType.DMA((2,)),
-            pltpu.SemaphoreType.DMA((2,)),
-            pltpu.SemaphoreType.DMA((2,)),
-            pltpu.SemaphoreType.DMA((8, CHUNKS)),
-            pltpu.SemaphoreType.DMA((8, CHUNKS)),
+            pltpu.SemaphoreType.DMA((3,)),
+            pltpu.SemaphoreType.DMA((2, ROWS)),
+            pltpu.SemaphoreType.DMA((8, ROWS)),
+            pltpu.SemaphoreType.DMA((8, ROWS)),
         ],
         compiler_params=pltpu.CompilerParams(
             collective_id=0, has_side_effects=True, vmem_limit_bytes=48 * 1024 * 1024

time: 45.1 us -> 40.2 us (0.89)
  the two profiles are of different devices: /device:TPU:1 before, /device:TPU:16 now
where the time goes in v3:
time: 40.2 us; the launch traced here: 40.1 us
  Pallas kernels  40.1 us (100%)
    pallas_call x1, Pallas kernels, on_device(): pl.pallas_call(gather_kernel, out_shape=(jax.ShapeDtypeStruct((depth, inp...  36.4 us
    pallas_call x1, Pallas kernels, on_device(): pl.pallas_call(correlate_kernel, out_shape=jax.ShapeDtypeStruct((2, 2, ro...  3.72 us

profile of v3, /device:TPU:16, one launch (start us, length us, event | category | flops | bytes accessed | tf_op | source)
XLA Modules:
  0.0 40.1 jit_solution(5534356719794926357)
XLA Ops:
  0.0 36.4 %shard_map.73 = (bf16[256,2048]{1,0:T(8,128)(2,1)S(1)}, bf16[4,512,256]{2,1,0:T(8,128)(2,1)S(1)}) custom-call(s32[32,256,128]{2,1,0:T(8,128)} %bitcast.5, f32[4,2048]{1,0:T(4,128)} %taper_hbm.1, s32[32,128]{1,0:T(8,128)} %gain_hbm.1, bf16[2,256,1024]{2,1,0:T(8,128)(2,1)} %constant.8.clone.table_hbm, bf16[2,128,128]{2,1,0:T(8,128)(2,1)} %constant.9.clone.select_hbm, ...), custom_call_target="tpu_custom_call" | custom-call | tf_op jit(solution)/shard_map/pallas_call | solution.py:441
  36.4 3.7 %shard_map.74 = bf16[2,2,512,2048]{3,2,1,0:T(8,128)(2,1)} custom-call(bf16[256,2048]{1,0:T(8,128)(2,1)S(1)} %get-tuple-element.7.signal_ref, bf16[4,512,256]{2,1,0:T(8,128)(2,1)S(1)} %get-tuple-element.8.left_ref), custom_call_target="tpu_custom_call" | custom-call | tf_op jit(solution)/shard_map/pallas_call | solution.py:478

commit v4 on v3

--- a/solution.py
+++ b/solution.py
@@ -25,6 +25,7 @@
 LANES = 128
 ROW = 8
 ROWS = SOURCES // ROW
+NEAR = 2
 PITCH = SPECS * POINTS // LANES + 8
 
 
@@ -81,8 +82,8 @@
 
 def gather_kernel(
     volt_hbm, taper_hbm, gain_hbm, table_hbm, select_hbm, permute_hbm, turns_hbm, out_ref, left_ref,
-    volts, taper_ref, gain_ref, table, select_ref, permute, turns, sums, halo_sums, stage, halo_out, halo_in, tiles, other, passing, gathered,
-    load_sem, const_sem, halo_sem, swap_send, swap_recv, ring_send, ring_recv,
+    volts, taper_ref, gain_ref, table, select_ref, permute, turns, sums, halo_sums, factors, stage, halo_out, halo_in, tiles, other, passing, gathered,
+    load_sem, const_sem, halo_sem, swap_send, swap_recv, spread_recv, ring_send, ring_recv,
 ):
     chan, feed = lax.axis_index("chan"), lax.axis_index("feed")
     core = lax.rem(chan, 2)
@@ -91,7 +92,6 @@
     high = 2 * feed + parity
     place = column * 2 + core
     line = lax.div(place, ROW)
-    near = pl.ds(pl.multiple_of(line * ROW, ROW), ROW)
 
     def level_of(level):
         return lax.rem(level + RING, RING)
@@ -116,14 +116,15 @@
     )
     copies = [pltpu.make_async_copy(*pair, const_sem.at[n]) for n, pair in enumerate(small)]
     taper_copy, table_copy, gain_copy, select_copy, permute_copy, turns_copy = copies
-    taper_copy.start()
+    for copy in (taper_copy, gain_copy, select_copy):
+        copy.start()
     for half in (1, 0):
         for part in range(2):
             load(half, part).start()
         if half == 1:
             table_copy.start()
-    for copy in copies[2:]:
-        copy.start()
+    permute_copy.start()
+    turns_copy.start()
 
     barrier = pltpu.get_barrier_semaphore()
 
@@ -190,6 +191,12 @@
         return wide[:LANES] + wide[LANES:] + narrow
 
     halo_sums[:, :, 3 * IN_DEV :] = jnp.zeros((2, 2, IN_DEV, HALF), BF16)
+    gain_copy.wait()
+    select_copy.wait()
+    gain_rows = jnp.concatenate([gain_ref[...].astype(F32).astype(BF16)] * 4, axis=0)
+
+    for which in range(2):
+        factors[which] = transposed_dot(select_ref[which], gain_rows) * (1.0 / 4096.0)
     taper_copy.wait()
     for part in range(2):
         load(1, part).wait()
@@ -211,12 +218,6 @@
     for part in range(2):
         load(0, part).wait()
         lax.fori_loop(0, HALF // LANES, functools.partial(main_step, part=part), 0)
-
-    gain_copy.wait()
-    select_copy.wait()
-    gain_rows = jnp.concatenate([gain_ref[...].astype(F32).astype(BF16)] * 4, axis=0)
-
-    factors = [transposed_dot(select_ref[which], gain_rows) * (1.0 / 4096.0) for which in range(2)]
 
     def settle(which, group, value):
         value = value * factors[which]
@@ -253,12 +254,15 @@
             device_id=device, device_id_type=MESH,
         )
 
+    def row_at(offset):
+        return lax.rem(line + offset + ROWS, ROWS) * ROW
+
     def far_row(step):
-        return lax.rem(line + step, ROWS) * ROW
+        return row_at(step - NEAR + 1)
 
     def held(step, origin, start=0, count=ROW):
-        if step == 0:
-            return passing.at[origin, pl.ds(start, count)]
+        if step < NEAR:
+            return passing.at[step, origin, pl.ds(start, count)]
         return gathered.at[origin, pl.ds(far_row(step) + start, count)]
 
     def part_of(slot):
@@ -272,8 +276,8 @@
         origin = level_of(high - {0: 0, 1: 0, 2: 1, 3: 2}[kind] * sign)
         if kind >= 2:
             source = held(step, origin, start, count)
-        elif step == 0:
-            source = tiles.at[lax.rem(parity + 1 + kind, 2), near]
+        elif step < NEAR:
+            source = tiles.at[lax.rem(parity + 1 + kind, 2), pl.ds(row_at(step), ROW)]
         elif kind == 0:
             source = other.at[pl.ds(far_row(step), ROW)]
         else:
@@ -297,62 +301,67 @@
             arrival(slot, step)
             send(slot + 4, step)
 
-    for slot in range(4):
-        send(slot, 0)
-
+    for step in range(NEAR):
+        for slot in range(4):
+            send(slot, step)
+
+    far_count = (ROWS - NEAR) * ROW
     for kind in range(2):
 
         def swap_step(step, _, kind=kind):
-            to = lax.rem((line + 1) * ROW + step, SOURCES)
+            to = lax.rem((line + NEAR) * ROW + step, SOURCES)
             source = tiles.at[lax.rem(parity + 1 + kind, 2), to]
             target = gathered.at[high, place] if kind else other.at[place]
             arrives = swap_recv.at[kind, ROWS - 1 - lax.div(step, ROW)]
             push(source, target, swap_send.at[kind], arrives, plane_at(to)).start()
             return 0
 
-        lax.fori_loop(0, SOURCES - ROW, swap_step, 0)
+        lax.fori_loop(0, far_count, swap_step, 0)
 
     def landed(kind, step):
         some = pl.ds(far_row(step), ROW)
         whole = gathered.at[high, some] if kind else other.at[some]
         pltpu.make_async_copy(whole, whole, swap_recv.at[kind, step]).wait()
 
-    def spread():
+    def spread(step):
         for slot in range(4, 8):
-            arrival(slot, 0)
-        own = pltpu.make_async_copy(tiles.at[parity, near], passing.at[high], swap_recv.at[0, 0])
+            arrival(slot, step)
+        own = tiles.at[parity, pl.ds(row_at(step), ROW)]
+        own = pltpu.make_async_copy(own, passing.at[step, high], spread_recv.at[step])
         own.start()
         own.wait()
 
-        def row_step(step, _):
-            index = lax.rem(place + step, ROW)
+        def row_step(index, _):
+            index = lax.rem(place + index, ROW)
             push(
-                passing.at[:, index], gathered.at[:, place],
-                swap_send.at[2], swap_recv.at[1, 0], plane_at(line * ROW + index),
+                passing.at[step, :, index], gathered.at[:, place],
+                swap_send.at[2 + step], swap_recv.at[step, 0], plane_at(row_at(step) + index),
             ).start()
             return 0
 
-        lax.fori_loop(1, ROW, row_step, 0)
-        pltpu.make_async_copy(
-            passing.at[:, lax.rem(place, ROW)], gathered.at[:, place], swap_recv.at[1, 0]
-        ).start()
+        lax.fori_loop(0 if step else 1, ROW, row_step, 0)
+        if step == 0:
+            pltpu.make_async_copy(
+                passing.at[0, :, lax.rem(place, ROW)], gathered.at[:, place], swap_recv.at[0, 0]
+            ).start()
+
+    def far(*steps):
+        for kind in range(2):
+            for step in steps:
+                landed(kind, step)
+                send(2 * kind, step)
+                send(2 * kind + 1, step)
 
     hand_on(0)
-    for kind in range(2):
-        for step in (1, 2):
-            landed(kind, step)
-            send(2 * kind, step)
-            send(2 * kind + 1, step)
-    spread()
-    for kind in range(2):
-        for step in (3,):
-            landed(kind, step)
-            send(2 * kind, step)
-            send(2 * kind + 1, step)
     hand_on(1)
+    far(2, 3)
+    spread(0)
+    spread(1)
     hand_on(2)
     hand_on(3)
-    pltpu.make_async_copy(gathered.at[:, near], gathered.at[:, near], swap_recv.at[1, 0]).wait()
+    for step in range(NEAR):
+        some = gathered.at[:, pl.ds(row_at(-step), ROW)]
+        pltpu.make_async_copy(some, some, swap_recv.at[step, 0]).wait()
 
     permute_copy.wait()
     turns_copy.wait()
@@ -388,20 +397,21 @@
     turn(0, feed)
     turn(1, feed - 1 + 2 * parity)
     prepare(0)
-    for step in range(1, ROWS):
+    for step in range(NEAR, ROWS):
         arrival(4, step)
         arrival(5, step)
     turn(2, feed + 1 - 2 * parity)
-    for step in range(1, ROWS):
+    for step in range(NEAR, ROWS):
         arrival(6, step)
         arrival(7, step)
     turn(3, feed + 2)
     prepare(1)
     for kind in range(2):
-        some = tiles.at[0, pl.ds(0, SOURCES - ROW)]
+        some = tiles.at[0, pl.ds(0, far_count)]
         pltpu.make_async_copy(some, some, swap_send.at[kind]).wait()
-    some = passing.at[:, pl.ds(0, ROW - 1)]
-    pltpu.make_async_copy(some, some, swap_send.at[2]).wait()
+    for step in range(NEAR):
+        some = passing.at[step, :, pl.ds(0, ROW if step else ROW - 1)]
+        pltpu.make_async_copy(some, some, swap_send.at[2 + step]).wait()
     for slot in range(8):
         for step in range(ROWS):
             ring(slot, step).wait_send()
@@ -456,18 +466,20 @@
             pltpu.VMEM(turns.shape, BF16),
             pltpu.VMEM((2, 2, SPECS * IN_DEV, HALF), BF16),
             pltpu.VMEM((2, 2, LANES, HALF), BF16),
+            pltpu.VMEM((2, LANES, LANES), F32),
             pltpu.VMEM((2 * SOURCES * TILE, LANES), F32),
             pltpu.VMEM((2, LANES, LANES), BF16),
             pltpu.VMEM((2, LANES, LANES), BF16),
             pltpu.VMEM((2, SOURCES, TILE, LANES), BF16),
             pltpu.VMEM((SOURCES, TILE, LANES), BF16),
-            pltpu.VMEM((RING, ROW, TILE, LANES), BF16),
+            pltpu.VMEM((NEAR, RING, ROW, TILE, LANES), BF16),
             pltpu.VMEM((RING, SOURCES, TILE, LANES), BF16),
             pltpu.SemaphoreType.DMA((2, 2)),
             pltpu.SemaphoreType.DMA((len(operands) - 1,)),
             pltpu.SemaphoreType.DMA((2,)),
-            pltpu.SemaphoreType.DMA((3,)),
+            pltpu.SemaphoreType.DMA((2 + NEAR,)),
             pltpu.SemaphoreType.DMA((2, ROWS)),
+            pltpu.SemaphoreType.DMA((NEAR,)),
             pltpu.SemaphoreType.DMA((8, ROWS)),
             pltpu.SemaphoreType.DMA((8, ROWS)),
         ],

time: 40.2 us -> 39.9 us (level)
  the two profiles are of different devices: /device:TPU:16 before, /device:TPU:1 now
where the time goes in v4:
time: 39.9 us
  Pallas kernels  39.8 us (100%)
    pallas_call x1, Pallas kernels, on_device(): pl.pallas_call(gather_kernel, out_shape=(jax.ShapeDtypeStruct((depth, inp...  36.1 us
    pallas_call x1, Pallas kernels, on_device(): pl.pallas_call(correlate_kernel, out_shape=jax.ShapeDtypeStruct((2, 2, ro...  3.72 us

profile of v4, /device:TPU:1, one launch (start us, length us, event | category | flops | bytes accessed | tf_op | source)
XLA Modules:
  0.0 39.9 jit_solution(4892893719553826055)
XLA Ops:
  0.0 36.1 %shard_map.73 = (bf16[256,2048]{1,0:T(8,128)(2,1)S(1)}, bf16[4,512,256]{2,1,0:T(8,128)(2,1)S(1)}) custom-call(s32[32,256,128]{2,1,0:T(8,128)} %bitcast.5, f32[4,2048]{1,0:T(4,128)} %taper_hbm.1, s32[32,128]{1,0:T(8,128)} %gain_hbm.1, bf16[2,256,1024]{2,1,0:T(8,128)(2,1)} %constant.8.clone.table_hbm, bf16[2,128,128]{2,1,0:T(8,128)(2,1)} %constant.9.clone.select_hbm, ...), custom_call_target="tpu_custom_call" | custom-call | tf_op jit(solution)/shard_map/pallas_call | solution.py:451
  36.1 3.7 %shard_map.74 = bf16[2,2,512,2048]{3,2,1,0:T(8,128)(2,1)} custom-call(bf16[256,2048]{1,0:T(8,128)(2,1)S(1)} %get-tuple-element.7.signal_ref, bf16[4,512,256]{2,1,0:T(8,128)(2,1)S(1)} %get-tuple-element.8.left_ref), custom_call_target="tpu_custom_call" | custom-call | tf_op jit(solution)/shard_map/pallas_call | solution.py:490

commit v5 on v4

--- a/solution.py
+++ b/solution.py
@@ -260,22 +260,21 @@
     def far_row(step):
         return row_at(step - NEAR + 1)
 
-    def held(step, origin, start=0, count=ROW):
+    def held(step, origin):
         if step < NEAR:
-            return passing.at[step, origin, pl.ds(start, count)]
-        return gathered.at[origin, pl.ds(far_row(step) + start, count)]
-
-    def part_of(slot):
-        return {6: (0, ROW // 2), 7: (ROW // 2, ROW // 2)}.get(slot, (0, ROW))
+            return passing.at[step, origin]
+        return gathered.at[origin, pl.ds(far_row(step), ROW)]
+
+    def used(slot, step):
+        return slot < 6 or slot - 6 == step % 2
 
     def ring(slot, step):
         sign = 1 if slot % 2 == 0 else -1
         kind = slot // 2
-        start, count = part_of(slot)
         hop = sign if kind == 0 else 2 * sign
         origin = level_of(high - {0: 0, 1: 0, 2: 1, 3: 2}[kind] * sign)
         if kind >= 2:
-            source = held(step, origin, start, count)
+            source = held(step, origin)
         elif step < NEAR:
             source = tiles.at[lax.rem(parity + 1 + kind, 2), pl.ds(row_at(step), ROW)]
         elif kind == 0:
@@ -283,14 +282,14 @@
         else:
             source = gathered.at[high, pl.ds(far_row(step), ROW)]
         return push(
-            source, held(step, origin, start, count),
+            source, held(step, origin),
             ring_send.at[slot, step], ring_recv.at[slot, step], ring_at(hop),
         )
 
     def arrival(slot, step):
         sign = 1 if slot % 2 == 0 else -1
         reach = {0: 1, 1: 2, 2: 3, 3: 4}[slot // 2]
-        target = held(step, level_of(high - reach * sign), *part_of(slot))
+        target = held(step, level_of(high - reach * sign))
         push(target, target, ring_send.at[slot, step], ring_recv.at[slot, step], ring_at(1)).wait_recv()
 
     def send(slot, step):
@@ -299,7 +298,8 @@
     def hand_on(step):
         for slot in range(4):
             arrival(slot, step)
-            send(slot + 4, step)
+            if used(slot + 4, step):
+                send(slot + 4, step)
 
     for step in range(NEAR):
         for slot in range(4):
@@ -325,7 +325,8 @@
 
     def spread(step):
         for slot in range(4, 8):
-            arrival(slot, step)
+            if used(slot, step):
+                arrival(slot, step)
         own = tiles.at[parity, pl.ds(row_at(step), ROW)]
         own = pltpu.make_async_copy(own, passing.at[step, high], spread_recv.at[step])
         own.start()
@@ -402,8 +403,7 @@
         arrival(5, step)
     turn(2, feed + 1 - 2 * parity)
     for step in range(NEAR, ROWS):
-        arrival(6, step)
-        arrival(7, step)
+        arrival(6 + step % 2, step)
     turn(3, feed + 2)
     prepare(1)
     for kind in range(2):
@@ -414,7 +414,8 @@
         pltpu.make_async_copy(some, some, swap_send.at[2 + step]).wait()
     for slot in range(8):
         for step in range(ROWS):
-            ring(slot, step).wait_send()
+            if used(slot, step):
+                ring(slot, step).wait_send()
 
     @pl.when(feed < RING // 2 - 1)
     def _():

time: 39.9 us -> 39.9 us (level)
  no operation moved by 1% of the time
where the time goes in v5:
time: 39.9 us; the launch traced here: 39.8 us
  Pallas kernels  39.8 us (100%)
    pallas_call x1, Pallas kernels, on_device(): pl.pallas_call(gather_kernel, out_shape=(jax.ShapeDtypeStruct((depth, inp...  36.1 us
    pallas_call x1, Pallas kernels, on_device(): pl.pallas_call(correlate_kernel, out_shape=jax.ShapeDtypeStruct((2, 2, ro...  3.72 us

profile of v5, /device:TPU:1, one launch (start us, length us, event | category | flops | bytes accessed | tf_op | source)
XLA Modules:
  0.0 39.8 jit_solution(11587914349270870651)
XLA Ops:
  0.0 36.1 %shard_map.73 = (bf16[256,2048]{1,0:T(8,128)(2,1)S(1)}, bf16[4,512,256]{2,1,0:T(8,128)(2,1)S(1)}) custom-call(s32[32,256,128]{2,1,0:T(8,128)} %bitcast.5, f32[4,2048]{1,0:T(4,128)} %taper_hbm.1, s32[32,128]{1,0:T(8,128)} %gain_hbm.1, bf16[2,256,1024]{2,1,0:T(8,128)(2,1)} %constant.8.clone.table_hbm, bf16[2,128,128]{2,1,0:T(8,128)(2,1)} %constant.9.clone.select_hbm, ...), custom_call_target="tpu_custom_call" | custom-call | tf_op jit(solution)/shard_map/pallas_call | solution.py:452
  36.1 3.7 %shard_map.74 = bf16[2,2,512,2048]{3,2,1,0:T(8,128)(2,1)} custom-call(bf16[256,2048]{1,0:T(8,128)(2,1)S(1)} %get-tuple-element.7.signal_ref, bf16[4,512,256]{2,1,0:T(8,128)(2,1)S(1)} %get-tuple-element.8.left_ref), custom_call_target="tpu_custom_call" | custom-call | tf_op jit(solution)/shard_map/pallas_call | solution.py:491

commit v6 on v4

--- a/solution.py
+++ b/solution.py
@@ -120,7 +120,7 @@
         copy.start()
     for half in (1, 0):
         for part in range(2):
-            load(half, part).start()
+            load(half, part).start(priority=part)
         if half == 1:
             table_copy.start()
     permute_copy.start()

time: 39.9 us -> 40.7 us (1.020)
  Pallas kernels: 39.8 us -> 40.6 us
    pallas_call x1, Pallas kernels: 36.1 us -> 36.9 us  [on_device(): pl.pallas_call(gather_kernel, out_shape=(jax.ShapeDtypeStruct((depth, inp...]
where the time goes in v6:
time: 40.7 us; the launch traced here: 40.6 us
  Pallas kernels  40.6 us (100%)
    pallas_call x1, Pallas kernels, on_device(): pl.pallas_call(gather_kernel, out_shape=(jax.ShapeDtypeStruct((depth, inp...  36.9 us
    pallas_call x1, Pallas kernels, on_device(): pl.pallas_call(correlate_kernel, out_shape=jax.ShapeDtypeStruct((2, 2, ro...  3.72 us

profile of v6, /device:TPU:1, one launch (start us, length us, event | category | flops | bytes accessed | tf_op | source)
XLA Modules:
  0.0 40.6 jit_solution(14703798911146691050)
XLA Ops:
  0.0 36.9 %shard_map.73 = (bf16[256,2048]{1,0:T(8,128)(2,1)S(1)}, bf16[4,512,256]{2,1,0:T(8,128)(2,1)S(1)}) custom-call(s32[32,256,128]{2,1,0:T(8,128)} %bitcast.5, f32[4,2048]{1,0:T(4,128)} %taper_hbm.1, s32[32,128]{1,0:T(8,128)} %gain_hbm.1, bf16[2,256,1024]{2,1,0:T(8,128)(2,1)} %constant.8.clone.table_hbm, bf16[2,128,128]{2,1,0:T(8,128)(2,1)} %constant.9.clone.select_hbm, ...), custom_call_target="tpu_custom_call" | custom-call | tf_op jit(solution)/shard_map/pallas_call | solution.py:451
  36.9 3.7 %shard_map.74 = bf16[2,2,512,2048]{3,2,1,0:T(8,128)(2,1)} custom-call(bf16[256,2048]{1,0:T(8,128)(2,1)S(1)} %get-tuple-element.7.signal_ref, bf16[4,512,256]{2,1,0:T(8,128)(2,1)S(1)} %get-tuple-element.8.left_ref), custom_call_target="tpu_custom_call" | custom-call | tf_op jit(solution)/shard_map/pallas_call | solution.py:490
